TPU v7x, 256 devices: a whole 4x4x8 slice. The times are simulated.
256 devices in a mesh: noise: 8 (over z), row: 16 (over y, x), col: 2 (over core).
Axes of the slice: x: 4, y: 4, z: 8, core: 2. Of those that a mesh axis runs over, the one named last changes fastest.
Arguments:
- images: bfloat16 [256, 4, 6144], P('row', None, 'col'), may hold values from -40 to 40
- gain: float32 [6144], P('col'), may hold values from 0.3 to 3.5
- up_weight: bfloat16 [6144, 12288], P('col', 'row'), may hold values from -0.078125 to 0.078125
- down_weight: bfloat16 [12288, 6144], P('row', 'col'), may hold values from -0.0546875 to 0.0546875
- cotangent: bfloat16 [256, 16, 6144], P('row', 'noise', 'col'), may hold values from -6 to 6
- seeds: int32 [16], P('noise'), may hold values from 0 to 999999
- assign: int32 [16, 1], replicated, may hold values from 0 to 3, as said below
Outputs:
- saliency: float32 [256, 4, 6144], P('row', None, 'col')
Inputs may be any that keep to these rules, and one draw needn't show every extreme that they name: `assign`: every one of the 4 images is named by at least one copy.
All inputs are finite; a program needn't handle non-finite values.
Results may differ from a plain program's by a relative error of at most 0.0019.
Values may be sent and summed in bfloat16 or wider, within the bound.
A program may use at most 64 MiB of HBM per device.

v0:
```python
import math
import jax
import jax.numpy as jnp
from jax import lax
from jax.sharding import PartitionSpec as P

D = 6144
noise_scale = 0.6
gelu_coef = 0.044715
root_term = math.sqrt(2.0 / math.pi)


def mix_noise(seed_value, token_index, feature_index, width):
    linear = token_index[:, None] * width + feature_index[None, :]
    mixed = linear * 1664525 + seed_value * 1013904223
    mixed = mixed ^ mixed >> 13
    mixed = mixed * 1274126177
    mixed = mixed ^ mixed >> 16
    return ((mixed & 65535).astype(jnp.float32) - 32767.5) * (1.0 / 18918.0)


def gelu_slope(preact):
    inner = root_term * (preact + gelu_coef * preact * preact * preact)
    tanh_val = jnp.tanh(inner)
    return 0.5 * (1.0 + tanh_val) + 0.5 * preact * (1.0 - tanh_val * tanh_val) * root_term * (
        1.0 + 3.0 * gelu_coef * preact * preact
    )


def body(images, gain, up_weight, down_weight, cotangent, seeds, assign):
    slot_count = seeds.shape[0]
    tok_local = images.shape[0]
    image_count = images.shape[1]
    width_local = images.shape[2]
    col_index = lax.axis_index("col")
    row_index = lax.axis_index("row")
    noise_index = lax.axis_index("noise")
    image_ids = jnp.arange(image_count, dtype=jnp.int32)
    my_images = lax.dynamic_slice_in_dim(assign[:, 0], noise_index * slot_count, slot_count)
    onehot = (my_images[:, None] == image_ids[None, :]).astype(jnp.float32)
    clean_rows = jnp.einsum(
        "si,tid->tsd", onehot.astype(jnp.bfloat16), images, preferred_element_type=jnp.float32
    )
    token_index = row_index * tok_local + jnp.arange(tok_local, dtype=jnp.int32)
    feature_index = col_index * width_local + jnp.arange(width_local, dtype=jnp.int32)
    noise_field = jax.vmap(
        lambda seed_value: mix_noise(seed_value, token_index, feature_index, D), out_axes=1
    )(seeds)
    noisy_rows = clean_rows + noise_scale * noise_field
    feat_mean = lax.psum(jnp.sum(noisy_rows, axis=-1), "col") / D
    centred = noisy_rows - feat_mean[..., None]
    feat_var = lax.psum(jnp.sum(centred * centred, axis=-1), "col") / D
    inv_std = lax.rsqrt(feat_var + 1e-06)[..., None]
    normed = centred * inv_std
    scaled = (normed * gain).astype(jnp.bfloat16)
    gathered = (
        lax.all_gather(scaled, "row", axis=0, tiled=True),
        lax.all_gather(cotangent, "row", axis=0, tiled=True),
    )
    row_count = gathered[0].shape[0] * slot_count
    full_scaled = gathered[0].reshape(row_count, width_local)
    full_cotangent = gathered[1].reshape(row_count, width_local)
    preact_part = jnp.dot(full_scaled, up_weight, preferred_element_type=jnp.float32)
    back_part = jnp.einsum(
        "td,hd->th", full_cotangent, down_weight, preferred_element_type=jnp.float32
    )
    preact, back_grad = lax.psum((preact_part, back_part), "col")
    hidden_grad = (back_grad * gelu_slope(preact)).astype(jnp.bfloat16)
    scaled_grad = lax.psum_scatter(
        jnp.einsum("th,dh->td", hidden_grad, up_weight, preferred_element_type=jnp.float32),
        "row",
        scatter_dimension=0,
        tiled=True,
    )
    scaled_grad = scaled_grad.reshape(tok_local, slot_count, width_local)
    normed_grad = scaled_grad * gain
    grad_sum, grad_dot = lax.psum(
        (jnp.sum(normed_grad, axis=-1), jnp.sum(normed_grad * normed, axis=-1)), "col"
    )
    input_grad = cotangent.astype(jnp.float32) + inv_std * (
        normed_grad - grad_sum[..., None] / D - normed * (grad_dot[..., None] / D)
    )
    partial_totals = jnp.einsum("si,tsd->tid", onehot, input_grad, precision=lax.Precision.HIGHEST)
    onehot_all = (assign[:, 0][:, None] == image_ids[None, :]).astype(jnp.float32)
    counts = jnp.sum(onehot_all, axis=0)
    totals = lax.psum(partial_totals, "noise")
    return totals / counts[None, :, None]


def solution(mesh):
    placed = (
        P("row", None, "col"),
        P("col"),
        P("col", "row"),
        P("row", "col"),
        P("row", "noise", "col"),
        P("noise"),
        P(),
    )
    return jax.shard_map(
        body, mesh=mesh, in_specs=placed, out_specs=P("row", None, "col"), check_vma=False
    )
```

profile of v0, /device:TPU:2, one launch (start us, length us, event | category | flops | bytes accessed | tf_op | source)
XLA Modules:
  0.0 361.4 jit_solution(3402559265118721403)
XLA Ops:
  6.6 0.7 broadcast_multiply_fusion.3
  7.3 0.7 dynamic-slice_bitcast_fusion
  8.1 0.9 fusion.41
  9.0 2.5 psum.49
  11.5 0.4 multiply_reduce_fusion.2
  11.8 2.5 psum.50
  14.3 1.0 multiply_convert_fusion
  15.4 0.7 all-gather.3.cloned.1.call-update
  16.1 54.5 %all-gather.5.cloned.1.call-done = bf16[256,2,3072]{2,1,0:T(2,128)(2,1)} async-done(((bf16[16,2,3072]{2,1,0:T(2,128)(2,1)}), bf16[256,2,3072]{2,1,0:T(2,128)(2,1)}) %all-gather.5.cloned.1.call-update) | async-done | bytes 3145744 | tf_op jit(solution)/shard_map/all_gather | solution.py:57
  70.6 7.5 %reshape.60 = bf16[512,3072]{1,0:T(8,128)(2,1)} reshape(bf16[256,2,3072]{2,1,0:T(2,128)(2,1)} %all-gather.5.cloned.1.call-done) | data formatting | bytes 6291456 | tf_op jit(solution)/shard_map/reshape | solution.py:61
  78.2 7.1 %fusion.43 = f32[512,768]{1,0:T(8,128)} fusion(bf16[512,3072]{1,0:T(8,128)(2,1)} %reshape.60, bf16[3072,768]{1,0:T(8,128)(2,1)} %param.9), kind=kOutput, calls=%fused_computation.66 | convolution fusion | flops 2415919104 | bytes 9437184 | tf_op jit(solution)/shard_map/dot_general | solution.py:63
  85.2 39.8 %all-gather.3.cloned.1.call-done = bf16[256,2,3072]{2,1,0:T(2,128)(2,1)} async-done(((bf16[16,2,3072]{2,1,0:T(2,128)(2,1)}), bf16[256,2,3072]{2,1,0:T(2,128)(2,1)}) %all-gather.3.cloned.1.call-update) | async-done | bytes 3145744 | tf_op jit(solution)/shard_map/all_gather | solution.py:58
  125.0 7.5 %reshape.59 = bf16[512,3072]{1,0:T(8,128)(2,1)} reshape(bf16[256,2,3072]{2,1,0:T(2,128)(2,1)} %all-gather.3.cloned.1.call-done) | data formatting | bytes 6291456 | tf_op jit(solution)/shard_map/reshape | solution.py:62
  132.6 7.1 %fusion.42 = f32[512,768]{1,0:T(8,128)} fusion(bf16[512,3072]{1,0:T(8,128)(2,1)} %reshape.59, bf16[768,3072]{1,0:T(8,128)(2,1)} %param.10), kind=kOutput, calls=%fused_computation.65 | convolution fusion | flops 2415919104 | bytes 9437184 | tf_op jit(solution)/shard_map/td,hd->th/dot_general | solution.py:64
  139.7 33.9 %all-reduce.7.cloned.1.call-done = (f32[512,768]{1,0:T(8,128)}, f32[512,768]{1,0:T(8,128)}) async-done(((f32[512,768]{1,0:T(8,128)}, f32[512,768]{1,0:T(8,128)}), (f32[512,768]{1,0:T(8,128)}, f32[512,768]{1,0:T(8,128)})) %all-reduce.7.cloned.1.call-update) | async-done | bytes 3145744 | tf_op jit(solution)/shard_map/psum | solution.py:67
  173.6 9.2 %fusion.8 = f32[512,3072]{1,0:T(8,128)} fusion(bf16[3072,768]{1,0:T(8,128)(2,1)} %param.9, f32[512,768]{1,0:T(8,128)} %get-tuple-element.7, f32[512,768]{1,0:T(8,128)} %get-tuple-element.8), kind=kOutput, calls=%fused_computation.12 | convolution fusion | flops 2423390208 | bytes 14155776 | tf_op jit(solution)/shard_map/th,dh->td/dot_general | solution.py:70
  182.8 0.2 all-reduce.5.cloned.1.call-start
  183.1 87.3 %reduce-scatter.2.cloned.1.call-done = f32[32,3072]{1,0:T(8,128)} async-done(((f32[512,3072]{1,0:T(8,128)}), f32[32,3072]{1,0:T(8,128)}) %reduce-scatter.2.cloned.1.call-update) | async-done | bytes 393232 | tf_op jit(solution)/shard_map/reduce_scatter | solution.py:69
  270.3 1.3 reshape.61
  271.6 0.5 multiply_reduce_fusion
  272.3 3.3 all-reduce
  275.7 2.3 convolution_bitcast_fusion
  278.1 74.4 %all-reduce.5.cloned.1.call-done = f32[16,4,3072]{2,1,0:T(4,128)} async-done(((f32[16,4,3072]{2,1,0:T(4,128)}), f32[16,4,3072]{2,1,0:T(4,128)}) %all-reduce.5.cloned.1.call-update) | async-done | bytes 786448 | tf_op jit(solution)/shard_map/psum | solution.py:86
  352.6 2.3 broadcast_divide_fusion
  (27 shorter events, 0.7 us)
Async XLA Ops:
  6.5 1.5 copy-start
  6.5 64.1 %all-gather.5.cloned.1.call-start = ((), (), s32[]{:S(2)}) async-start(), calls=%async_computation.2 | async-start | bytes 3342336 | tf_op jit(solution)/shard_map/all_gather | solution.py:57
  8.1 6.2 %copy-start.3 = (f32[3072]{0:T(1024)S(1)}, f32[3072]{0:T(1024)}, u32[]{:S(2)}) copy-start(f32[3072]{0:T(1024)} %param.8) | copy-start | bytes 36868
  15.3 109.7 %all-gather.3.cloned.1.call-start = ((), (), s32[]{:S(2)}) async-start(), calls=%async_computation.1 | async-start | bytes 3342336 | tf_op jit(solution)/shard_map/all_gather | solution.py:58
  16.1 157.5 %all-reduce.7.cloned.1.call-start = ((), (), s32[]{:S(2)}) async-start(), calls=%async_computation.5 | async-start | bytes 6291456 | tf_op jit(solution)/shard_map/psum | solution.py:67
  139.7 130.7 %reduce-scatter.2.cloned.1.call-start = ((), (), s32[]{:S(2)}) async-start(), calls=%async_computation.3 | async-start | bytes 6684672 | tf_op jit(solution)/shard_map/reduce_scatter | solution.py:69
  182.8 92.8 %copy-start.2 = (bf16[16,2,3072]{2,1,0:T(2,128)(2,1)S(1)}, bf16[16,2,3072]{2,1,0:T(2,128)(2,1)}, u32[]{:S(2)}) copy-start(bf16[16,2,3072]{2,1,0:T(2,128)(2,1)} %param.11) | copy-start | bytes 589828
  182.8 169.7 %all-reduce.5.cloned.1.call-start = ((), (), s32[]{:S(2)}) async-start(), calls=%async_computation.4 | async-start | bytes 1572864 | tf_op jit(solution)/shard_map/psum | solution.py:86
  270.3 1.8 copy-start.1
  275.7 2.4 copy-start.4
Sparse Core Ops, SparseCore 0:
  15.4 55.1 all-gather.4
  73.1 51.9 all-gather.2
  139.8 33.7 all-reduce.6
  182.9 87.3 reduce-scatter.1
  278.1 74.3 all-reduce.4
where the time goes:
time: 362 us; the launch traced here: 361 us
  waiting for transfers between devices  291 us (80%)
  matrix products  26.6 us (7%)
  local copies, waits for them, and re-layouts  17.2 us (5%)
  between operations  13.2 us (4%)
  blocking collectives  8.21 us (2%)
  other arithmetic  5.16 us (1%)
    reduce_scatter x1, waiting for transfers between devices, body(): lax.psum_scatter(jnp.einsum('th,dh->td', hidden_grad, up_weight, preferre...  87.3 us
    psum x1, waiting for transfers between devices, body(): totals = lax.psum(partial_totals, 'noise')  74.4 us
    all_gather x1, waiting for transfers between devices, body(): lax.all_gather(scaled, 'row', axis=0, tiled=True)  54.5 us
    all_gather x1, waiting for transfers between devices, body(): lax.all_gather(cotangent, 'row', axis=0, tiled=True)  39.8 us
    psum x1, waiting for transfers between devices, body(): preact, back_grad = lax.psum((preact_part, back_part), 'col')  33.9 us
    dot_general x1, matrix products, body(): jnp.einsum('th,dh->td', hidden_grad, up_weight, preferred_element_type=jn...  9.19 us
    reshape x1, local copies, waits for them, and re-layouts, body(): full_scaled = gathered[0].reshape(row_count, width_local)  7.54 us
    reshape x1, local copies, waits for them, and re-layouts, body(): full_cotangent = gathered[1].reshape(row_count, width_local)  7.51 us
  transfers between devices with their start and end apart: 5, of which 5 were waited for; matrix products, arithmetic and copies ran while one was open for 4% of the time, Pallas kernels for 0%

commit v1 on v0

--- a/solution.py
+++ b/solution.py
@@ -55,7 +55,9 @@
     scaled = (normed * gain).astype(jnp.bfloat16)
     gathered = (
         lax.all_gather(scaled, "row", axis=0, tiled=True),
-        lax.all_gather(cotangent, "row", axis=0, tiled=True),
+        jnp.concatenate(
+            lax.all_to_all(jnp.stack([cotangent] * lax.axis_size("row")), "row", 0, 0), axis=0
+        ),
     )
     row_count = gathered[0].shape[0] * slot_count
     full_scaled = gathered[0].reshape(row_count, width_local)

time: 362 us -> 324 us (0.90)
  waiting for transfers between devices: 291 us -> 208 us
  blocking collectives: 8.21 us -> 57.3 us
    all_to_all x0 -> x1, blocking collectives: none -> 49 us  [body(): lax.all_to_all(jnp.stack([cotangent] * lax.axis_size('row')), 'row', 0, 0)]
    all_gather x1, waiting for transfers between devices: 54.5 us -> 12.7 us  [body(): lax.all_gather(scaled, 'row', axis=0, tiled=True)]
    all_gather x1 -> x0, waiting for transfers between devices: 39.8 us -> none  [body(): lax.all_gather(cotangent, 'row', axis=0, tiled=True)]
    reshape x1 -> x0, local copies, waits for them, and re-layouts: 7.51 us -> none  [body(): full_cotangent = gathered[1].reshape(row_count, width_local)]
    another operation x0 -> x2, local copies, waits for them, and re-layouts: none -> 5.13 us  [the longest x1 2.71 us: body(): full_cotangent = gathered[1].reshape(row_count, width_local)]
  transfers between devices with their start and end apart: 5 -> 4, of which waited for: 5 -> 4; matrix products, arithmetic and copies ran while one was open for 4% -> 4% of each run, Pallas kernels for 0% -> 0%
where the time goes in v1:
time: 324 us
  waiting for transfers between devices  208 us (64%)
  blocking collectives  57.3 us (18%)
  matrix products  25.6 us (8%)
  local copies, waits for them, and re-layouts  13.6 us (4%)
  between operations  13.3 us (4%)
  other arithmetic  5.15 us (2%)
    reduce_scatter x1, waiting for transfers between devices, body(): lax.psum_scatter(jnp.einsum('th,dh->td', hidden_grad, up_weight, preferre...  87.4 us
    psum x1, waiting for transfers between devices, body(): totals = lax.psum(partial_totals, 'noise')  74.4 us
    all_to_all x1, blocking collectives, body(): lax.all_to_all(jnp.stack([cotangent] * lax.axis_size('row')), 'row', 0, 0)  49 us
    psum x1, waiting for transfers between devices, body(): preact, back_grad = lax.psum((preact_part, back_part), 'col')  33.7 us
    all_gather x1, waiting for transfers between devices, body(): lax.all_gather(scaled, 'row', axis=0, tiled=True)  12.7 us
    dot_general x1, matrix products, body(): jnp.einsum('th,dh->td', hidden_grad, up_weight, preferred_element_type=jn...  9.19 us
    dot_general x1, matrix products, body(): jnp.einsum('td,hd->th', full_cotangent, down_weight, preferred_element_ty...  7.08 us
  transfers between devices with their start and end apart: 4, of which 4 were waited for; matrix products, arithmetic and copies ran while one was open for 4% of the time, Pallas kernels for 0%

profile of v1, /device:TPU:2, one launch (start us, length us, event | category | flops | bytes accessed | tf_op | source)
XLA Modules:
  0.0 323.5 jit_solution(8634527289678298368)
XLA Ops:
  6.6 0.7 broadcast_multiply_fusion.3
  7.3 0.7 dynamic-slice_bitcast_fusion
  8.1 0.9 fusion.41
  9.0 2.5 psum.49
  11.5 0.4 multiply_reduce_fusion.2
  11.9 2.5 psum.50
  14.3 1.0 multiply_convert_fusion
  15.4 2.4 stack.2
  17.8 49.0 %all_to_all.5 = bf16[16,16,2,3072]{3,2,1,0:T(2,128)(2,1)S(1)} all-to-all(bf16[16,16,2,3072]{3,2,1,0:T(2,128)(2,1)S(1)} %stack.2), channel_id=1, replica_groups=mesh['noise'=8,'row'=16,'col'=2] {'row'}, dimensions={0} | all-to-all | bytes 6291456 | tf_op jit(solution)/shard_map/all_to_all | solution.py:59
  66.9 2.7 reshape_reshape.3
  69.6 7.1 %fusion.42 = f32[512,768]{1,0:T(8,128)} fusion(bf16[512,3072]{1,0:T(8,128)(2,1)} %reshape_reshape.3, bf16[768,3072]{1,0:T(8,128)(2,1)} %param.10), kind=kOutput, calls=%fused_computation.65 | convolution fusion | flops 2415919104 | bytes 9437184 | tf_op jit(solution)/shard_map/td,hd->th/dot_general | solution.py:66
  76.7 12.7 %all-gather.2.cloned.1.call-done = bf16[256,2,3072]{2,1,0:T(2,128)(2,1)} async-done(((bf16[16,2,3072]{2,1,0:T(2,128)(2,1)}), bf16[256,2,3072]{2,1,0:T(2,128)(2,1)}) %all-gather.2.cloned.1.call-update) | async-done | bytes 3145744 | tf_op jit(solution)/shard_map/all_gather | solution.py:57
  89.4 6.3 %reshape.58 = bf16[512,3072]{1,0:T(8,128)(2,1)S(1)} reshape(bf16[256,2,3072]{2,1,0:T(2,128)(2,1)} %all-gather.2.cloned.1.call-done) | data formatting | bytes 6291456 | tf_op jit(solution)/shard_map/reshape | solution.py:63
  95.7 6.1 %fusion.43 = f32[512,768]{1,0:T(8,128)} fusion(bf16[512,3072]{1,0:T(8,128)(2,1)S(1)} %reshape.58, bf16[3072,768]{1,0:T(8,128)(2,1)} %param.9), kind=kOutput, calls=%fused_computation.66 | convolution fusion | flops 2415919104 | bytes 9437184 | tf_op jit(solution)/shard_map/dot_general | solution.py:65
  101.8 0.2 reduce-scatter.2.cloned.1.call-start
  102.1 33.7 %all-reduce.7.cloned.1.call-done = (f32[512,768]{1,0:T(8,128)}, f32[512,768]{1,0:T(8,128)}) async-done(((f32[512,768]{1,0:T(8,128)}, f32[512,768]{1,0:T(8,128)}), (f32[512,768]{1,0:T(8,128)}, f32[512,768]{1,0:T(8,128)})) %all-reduce.7.cloned.1.call-update) | async-done | bytes 3145744 | tf_op jit(solution)/shard_map/psum | solution.py:69
  135.8 9.2 %fusion.8 = f32[512,3072]{1,0:T(8,128)} fusion(bf16[3072,768]{1,0:T(8,128)(2,1)} %param.9, f32[512,768]{1,0:T(8,128)} %get-tuple-element.7, f32[512,768]{1,0:T(8,128)} %get-tuple-element.8), kind=kOutput, calls=%fused_computation.12 | convolution fusion | flops 2423390208 | bytes 14155776 | tf_op jit(solution)/shard_map/th,dh->td/dot_general | solution.py:72
  145.1 87.4 %reduce-scatter.2.cloned.1.call-done = f32[32,3072]{1,0:T(8,128)} async-done(((f32[512,3072]{1,0:T(8,128)}), f32[32,3072]{1,0:T(8,128)}) %reduce-scatter.2.cloned.1.call-update) | async-done | bytes 393232 | tf_op jit(solution)/shard_map/reduce_scatter | solution.py:71
  232.5 1.3 reshape.59
  233.8 0.5 multiply_reduce_fusion
  234.5 3.3 %all-reduce = (f32[16,2]{1,0:T(8,128)S(1)}, f32[16,2]{1,0:T(8,128)S(1)}) all-reduce(f32[16,2]{1,0:T(8,128)S(1)} %multiply_reduce_fusion, f32[16,2]{1,0:T(8,128)S(1)} %reduce_sum.50), channel_id=1, replica_groups=mesh['noise'=8,'row'=16,'col'=2] {'col'}, use_global_device_ids=true, to_apply=%region_10.0 | all-reduce | flops 64 | bytes 512 | tf_op jit(solution)/shard_map/psum | solution.py:79
  237.9 2.3 convolution_bitcast_fusion
  240.3 74.4 %all-reduce.5.cloned.1.call-done = f32[16,4,3072]{2,1,0:T(4,128)} async-done(((f32[16,4,3072]{2,1,0:T(4,128)}), f32[16,4,3072]{2,1,0:T(4,128)}) %all-reduce.5.cloned.1.call-update) | async-done | bytes 786448 | tf_op jit(solution)/shard_map/psum | solution.py:88
  314.7 2.3 broadcast_divide_fusion
  (38 shorter events, 0.7 us)
Async XLA Ops:
  6.5 1.5 copy-start
  6.5 82.9 %all-gather.2.cloned.1.call-start = ((), (), s32[]{:S(2)}) async-start(), calls=%async_computation.2 | async-start | bytes 3342336 | tf_op jit(solution)/shard_map/all_gather | solution.py:57
  8.0 1.0 copy-start.9
  8.1 6.3 %copy-start.6 = (f32[3072]{0:T(1024)S(1)}, f32[3072]{0:T(1024)}, u32[]{:S(2)}) copy-start(f32[3072]{0:T(1024)} %param.8) | copy-start | bytes 36868
  8.1 7.3 %copy-start.4 = (bf16[16,2,3072]{2,1,0:T(2,128)(2,1)S(1)}, bf16[16,2,3072]{2,1,0:T(2,128)(2,1)}, u32[]{:S(2)}) copy-start(bf16[16,2,3072]{2,1,0:T(2,128)(2,1)} %param.11) | copy-start | bytes 589828
  9.0 6.4 %copy-start.1 = (f32[16,2,3072]{2,1,0:T(2,128)}, f32[16,2,3072]{2,1,0:T(2,128)S(1)}, u32[]{:S(2)}) copy-start(f32[16,2,3072]{2,1,0:T(2,128)S(1)} %get-tuple-element.10) | copy-start | bytes 1179652
  15.3 120.4 %all-reduce.7.cloned.1.call-start = ((), (), s32[]{:S(2)}) async-start(), calls=%async_computation.5 | async-start | bytes 6291456 | tf_op jit(solution)/shard_map/psum | solution.py:69
  101.8 130.7 %reduce-scatter.2.cloned.1.call-start = ((), (), s32[]{:S(2)}) async-start(), calls=%async_computation.3 | async-start | bytes 6684672 | tf_op jit(solution)/shard_map/reduce_scatter | solution.py:71
  145.0 88.8 %copy-start.2 = (f32[16,2,3072]{2,1,0:T(2,128)S(1)}, f32[16,2,3072]{2,1,0:T(2,128)}, u32[]{:S(2)}) copy-start(f32[16,2,3072]{2,1,0:T(2,128)} %copy-done.1) | copy-start | bytes 1179652
  145.0 88.9 %copy-start.7 = (f32[3072]{0:T(1024)S(1)}, f32[3072]{0:T(1024)}, u32[]{:S(2)}) copy-start(f32[3072]{0:T(1024)} %param.8) | copy-start | bytes 36868
  145.0 92.8 %copy-start.5 = (bf16[16,2,3072]{2,1,0:T(2,128)(2,1)S(1)}, bf16[16,2,3072]{2,1,0:T(2,128)(2,1)}, u32[]{:S(2)}) copy-start(bf16[16,2,3072]{2,1,0:T(2,128)(2,1)} %param.11) | copy-start | bytes 589828
  145.0 92.8 %copy-start.10 = (s32[2]{0:T(128)S(1)}, s32[2]{0:T(128)}, u32[]{:S(2)}) copy-start(s32[2]{0:T(128)} %copy-done.9) | copy-start | bytes 28
  145.0 169.7 %all-reduce.5.cloned.1.call-start = ((), (), s32[]{:S(2)}) async-start(), calls=%async_computation.4 | async-start | bytes 1572864 | tf_op jit(solution)/shard_map/psum | solution.py:88
  232.5 1.8 copy-start.3
  237.9 2.4 copy-start.8
Sparse Core Ops, SparseCore 0:
  15.5 73.8 all-gather.1
  102.0 33.7 all-reduce.6
  145.1 87.3 reduce-scatter.1
  240.3 74.3 all-reduce.4
